TPU v7x, 512 devices: a whole 4x8x8 slice. The times are simulated.
512 devices in a mesh: row: 64 (over z, x, core), col: 8 (over y).
Axes of the slice: x: 4, y: 8, z: 8, core: 2. Of those that a mesh axis runs over, the one named last changes fastest.
Arguments:
- tokens: bfloat16 [512, 8192], P('row', 'col'), may hold values from -6 to 6
- out_grad: bfloat16 [512, 8192], P('row', 'col'), may hold values from -6 to 6
- w_gate: bfloat16 [14336, 8192], P('row', 'col'), may hold values from -0.125 to 0.125
- w_up: bfloat16 [14336, 8192], P('row', 'col'), may hold values from -0.125 to 0.125
- w_down: bfloat16 [14336, 8192], P('row', 'col'), may hold values from -0.09375 to 0.09375
- mask_gate: int32 [112, 64], replicated, may hold values 0 or 1
- mask_up: int32 [112, 64], replicated, may hold values 0 or 1
- mask_down: int32 [112, 64], replicated, may hold values 0 or 1
Outputs:
- grad_tokens: bfloat16 [512, 8192], P('row', 'col')
- grad_gate: bfloat16 [14336, 8192], P('row', 'col')
- grad_up: bfloat16 [14336, 8192], P('row', 'col')
- grad_down: bfloat16 [14336, 8192], P('row', 'col')
All inputs are finite; a program needn't handle non-finite values.
Results may differ from a plain program's by a relative error of at most 0.005.
Values may be sent and summed in bfloat16 or wider, within the bound.
A program may use at most 64 MiB of HBM per device.

v0:
```python
import jax
import jax.numpy as jnp
from jax import lax
from jax.sharding import PartitionSpec as P

BLOCK = 128


def selector(start, count, blocks):
    index = start + jnp.arange(count, dtype=jnp.int32)
    owner = index // BLOCK
    return (owner[:, None] == jnp.arange(blocks, dtype=jnp.int32)[None, :]).astype(jnp.float32)


def expand(mask, row_start, rows, col_start, cols):
    left = selector(row_start, rows, mask.shape[0])
    right = selector(col_start, cols, mask.shape[1])
    inner = jnp.dot(left, mask.astype(jnp.float32))
    return jnp.dot(inner, right.T)


def gradients(gate, upper, dhidden):
    sig = jax.nn.sigmoid(gate)
    hidden = (gate * sig * upper).astype(jnp.bfloat16)
    dup = (dhidden * gate * sig).astype(jnp.bfloat16)
    dgate = (dhidden * upper * sig * (1.0 + gate * (1.0 - sig))).astype(jnp.bfloat16)
    return (hidden, dgate, dup)


def shards(tokens, out_grad, w_gate, w_up, w_down, mask_gate, mask_up, mask_down):
    row_pos = lax.axis_index("row")
    col_pos = lax.axis_index("col")
    unit_dev, feat_dev = w_gate.shape
    feat_start = col_pos * feat_dev
    unit_start = row_pos * unit_dev
    keep_gate = expand(mask_gate, unit_start, unit_dev, feat_start, feat_dev)
    keep_up = expand(mask_up, unit_start, unit_dev, feat_start, feat_dev)
    keep_down = expand(mask_down, unit_start, unit_dev, feat_start, feat_dev)
    gate_eff = (w_gate * keep_gate).astype(jnp.bfloat16)
    up_eff = (w_up * keep_up).astype(jnp.bfloat16)
    down_eff = (w_down * keep_down).astype(jnp.bfloat16)
    pair_eff = jnp.concatenate([gate_eff, up_eff], axis=0)
    all_tokens, all_grads = (
        lax.all_gather(tokens, "row", axis=0, tiled=True),
        lax.all_gather(out_grad, "row", axis=0, tiled=True),
    )
    partial_value = lax.dot_general(
        all_tokens, pair_eff, (((1,), (1,)), ((), ())), preferred_element_type=jnp.float32
    )
    dpartial = lax.dot_general(
        all_grads, down_eff, (((1,), (1,)), ((), ())), preferred_element_type=jnp.float32
    )
    summed, dsummed = lax.psum((partial_value, dpartial), "col")
    hidden, dgate, dup = gradients(summed[:, :unit_dev], summed[:, unit_dev:], dsummed)
    dpair = jnp.concatenate([dgate, dup], axis=1)
    grad_down = (
        lax.dot_general(
            hidden, all_grads, (((0,), (0,)), ((), ())), preferred_element_type=jnp.float32
        )
        * keep_down
    ).astype(jnp.bfloat16)
    grad_pair = lax.dot_general(
        dpair, all_tokens, (((0,), (0,)), ((), ())), preferred_element_type=jnp.float32
    )
    grad_gate = (grad_pair[:unit_dev] * keep_gate).astype(jnp.bfloat16)
    grad_up = (grad_pair[unit_dev:] * keep_up).astype(jnp.bfloat16)
    grad_tokens = lax.psum_scatter(
        jnp.dot(dpair, pair_eff, preferred_element_type=jnp.float32),
        "row",
        scatter_dimension=0,
        tiled=True,
    ).astype(jnp.bfloat16)
    return (grad_tokens, grad_gate, grad_up, grad_down)


def solution(mesh):
    return jax.shard_map(
        shards,
        mesh=mesh,
        in_specs=(
            P("row", "col"),
            P("row", "col"),
            P("row", "col"),
            P("row", "col"),
            P("row", "col"),
            P(),
            P(),
            P(),
        ),
        out_specs=(P("row", "col"), P("row", "col"), P("row", "col"), P("row", "col")),
        check_vma=False,
    )
```

profile of v0, /device:TPU:1, one launch (start us, length us, event | category | flops | bytes accessed | tf_op | source)
XLA Modules:
  0.0 548.0 jit_solution(4557731787975580544)
XLA Ops:
  7.2 0.0 copy-start.4
  7.2 0.0 copy-start.2
  7.2 0.0 all-gather.3.cloned.1.call-start
  7.2 0.7 all-gather.3.cloned.1.call-update
  7.9 0.0 all-gather.5.cloned.1.call-start
  8.0 0.7 all-gather.5.cloned.1.call-update
  8.7 0.0 all-reduce.5.cloned.1.call-start
  8.8 1.2 fusion.7
  10.0 2.3 multiply_convert_fusion
  12.2 0.0 copy-done.4
  12.2 0.0 copy-done.2
  12.2 1.2 multiply_convert_fusion.1
  13.5 0.0 copy-start.3
  13.5 86.3 %all-gather.3.cloned.1.call-done = bf16[512,1024]{1,0:T(8,128)(2,1)} async-done(((bf16[8,1024]{1,0:T(8,128)(2,1)}), bf16[512,1024]{1,0:T(8,128)(2,1)}) %all-gather.3.cloned.1.call-update) | async-done | bytes 1048592 | tf_op jit(solution)/shard_map/all_gather | solution.py:45
  99.8 2.6 convolution_bitcast_fusion.1
  102.4 80.5 %all-gather.5.cloned.1.call-done = bf16[512,1024]{1,0:T(8,128)(2,1)} async-done(((bf16[8,1024]{1,0:T(8,128)(2,1)}), bf16[512,1024]{1,0:T(8,128)(2,1)}) %all-gather.5.cloned.1.call-update) | async-done | bytes 1048592 | tf_op jit(solution)/shard_map/all_gather | solution.py:44
  182.9 0.0 copy-done.3
  182.9 3.0 convolution_bitcast_fusion
  185.9 0.0 all-reduce.5.cloned.1.call-update
  185.9 1.3 dynamic-slice
  187.8 74.4 %all-reduce.5.cloned.1.call-done = (f32[512,224]{0,1:T(8,128)}, f32[512,448]{0,1:T(8,128)}) async-done(((f32[512,224]{0,1:T(8,128)}, f32[512,448]{0,1:T(8,128)}), (f32[512,224]{0,1:T(8,128)}, f32[512,448]{0,1:T(8,128)})) %all-reduce.5.cloned.1.call-update) | async-done | bytes 1376272 | tf_op jit(solution)/shard_map/psum | solution.py:53
  262.2 1.6 multiply_convert_fusion.6
  263.8 3.2 fusion.12
  267.0 268.2 %all-reduce.6 = bf16[512,1024]{1,0:T(8,128)(2,1)} all-reduce(f32[512,1024]{1,0:T(8,128)} %fusion.12), channel_id=2, replica_groups=mesh['row'=64,'col'=8] {'row'}, use_global_device_ids=true, to_apply=%region_2.3.clone | all-reduce | flops 524288 | bytes 3145728
  535.2 1.3 dynamic-slice_convert_fusion
  536.6 1.9 fusion.13
  538.4 0.0 copy-start
  538.4 0.0 copy-start.1
  538.5 1.2 fusion.10
  539.6 0.1 copy-done
  539.7 0.6 copy-done.1
  540.3 1.2 fusion
  (2 shorter events, 0.0 us)
Async XLA Ops:
  7.2 5.1 copy-start.4
  7.2 5.1 copy-start.2
  7.2 92.6 %all-gather.3.cloned.1.call-start = ((), (), s32[]{:S(2)}) async-start(), calls=%async_computation | async-start | bytes 1064960 | tf_op jit(solution)/shard_map/all_gather | solution.py:45
  7.9 175.0 %all-gather.5.cloned.1.call-start = ((), (), s32[]{:S(2)}) async-start(), calls=%async_computation.1 | async-start | bytes 1064960 | tf_op jit(solution)/shard_map/all_gather | solution.py:44
  8.7 253.6 %all-reduce.5.cloned.1.call-start = ((), (), s32[]{:S(2)}) async-start(), calls=%async_computation.2 | async-start | bytes 2752512 | tf_op jit(solution)/shard_map/psum | solution.py:53
  13.5 169.4 %copy-start.3 = (bf16[224,1024]{1,0:T(8,128)(2,1)S(1)}, bf16[224,1024]{1,0:T(8,128)(2,1)}, u32[]{:S(2)}) copy-start(bf16[224,1024]{1,0:T(8,128)(2,1)} %get-tuple-element.10) | copy-start | bytes 1376260
  538.4 1.3 copy-start
  538.4 1.8 copy-start.1
Sparse Core Ops, SparseCore 0:
  11.4 88.3 all-gather.2
  103.1 79.7 all-gather.4
  186.0 76.1 all-reduce.4
where the time goes:
time: 552 us; the launch traced here: 548 us
  blocking collectives  268 us (49%)
  waiting for transfers between devices  243 us (44%)
  matrix products  16.6 us (3%)
  between operations  14.5 us (3%)
    unnamed x1, blocking collectives  268 us
    all_gather x1, waiting for transfers between devices, shards(): lax.all_gather(out_grad, 'row', axis=0, tiled=True)  86.3 us
    all_gather x1, waiting for transfers between devices, shards(): lax.all_gather(tokens, 'row', axis=0, tiled=True)  80.5 us
    psum x1, waiting for transfers between devices, shards(): summed, dsummed = lax.psum((partial_value, dpartial), 'col')  74.4 us
  transfers between devices with their start and end apart: 3, of which 3 were waited for; matrix products, arithmetic and copies ran while one was open for 2% of the time, Pallas kernels for 0%

commit v1 on v0

v1 whole, which is shorter than its diff:
```python
import jax
import jax.numpy as jnp
from jax import lax
from jax.experimental import pallas as pl
from jax.experimental.pallas import tpu as pltpu
from jax.sharding import PartitionSpec as P

BLOCK = 128
NZ, NX, NY = 8, 4, 8
UNITS, FEATS, PAD = 224, 1024, 256
WIDE = 3 * PAD
GROUPS = ((0, 1), (-1, 2), (-2, 3), (-3, 4))
F32, BF16 = jnp.float32, jnp.bfloat16


def expand(mask, row_start, col_start):
    blocks, wide = mask.shape
    unit = (row_start + lax.broadcasted_iota(jnp.int32, (UNITS, blocks), 0)) >> 7
    left = (unit == lax.broadcasted_iota(jnp.int32, (UNITS, blocks), 1)).astype(F32).astype(BF16)
    feat = (col_start + lax.broadcasted_iota(jnp.int32, (wide, FEATS), 1)) >> 7
    right = (feat == lax.broadcasted_iota(jnp.int32, (wide, FEATS), 0)).astype(F32).astype(BF16)
    inner = jnp.dot(left, mask.astype(F32).astype(BF16), preferred_element_type=F32)
    return jnp.dot(inner.astype(BF16), right, preferred_element_type=F32)


def kernel(
    tok, grd, wg, wu, wd, mg, mu, md,
    o_t, o_g, o_u, o_d,
    tokv, grdv, wv, mv, G, WE, KEEP, TOKS, GRDS, P32,
    SP, SM, S2, RP, RM, R2, SA, SB, RA, RB, D, GTS, GR, XS, XR, KX, ZS, ZR, ZO,
    lsem, xs_s, xs_r, z_s, z_r, c_s, c_r, y1_s, y1_r, y2_s, y2_r, d_s, d_r, e_s, e_r,
    g_s, g_r, h_s, h_r, k_s, k_r,
):
    row, y = lax.axis_index("row"), lax.axis_index("col")
    c = lax.rem(row, 2)
    x = lax.rem(row // 2, NX)
    z = row // (2 * NX)

    def zi(d):
        return lax.rem(z + (d + NZ), NZ)

    def xi(d):
        return lax.rem(x + (d + NX), NX)

    def yi(d):
        return lax.rem(y + (d + NY), NY)

    def dev(dz=0, dx=0, dc=0, dy=0):
        return ((zi(dz) * NX + xi(dx)) * 2 + lax.rem(c + dc, 2), yi(dy))

    sends = []

    def send(src, dst, ssem, rsem, where):
        cp = pltpu.make_async_remote_copy(
            src, dst, ssem, rsem, device_id=where, device_id_type=pl.DeviceIdType.MESH
        )
        cp.start()
        sends.append(cp)

    def arrived(dst, ssem, rsem):
        pltpu.make_async_remote_copy(
            dst, dst, ssem, rsem, device_id=dev(dc=1), device_id_type=pl.DeviceIdType.MESH
        ).wait_recv()

    peers = (
        [dev(dc=1)]
        + [dev(dx=k) for k in (1, 2, 3)]
        + [dev(dz=k) for k in (1, 2, 3, 4, 5, 6, 7)]
        + [dev(dy=k) for k in (1, 2, -1, -2)]
    )
    barrier = pltpu.get_barrier_semaphore()
    for p in peers:
        pl.semaphore_signal(barrier, inc=1, device_id=p, device_id_type=pl.DeviceIdType.MESH)
    loads = [
        pltpu.make_async_copy(s, d, lsem.at[i])
        for i, (s, d) in enumerate(
            (
                (tok, tokv), (grd, grdv),
                (mg, mv.at[0]), (mu, mv.at[1]), (md, mv.at[2]),
                (wg, wv.at[0]), (wu, wv.at[1]), (wd, wv.at[2]),
            )
        )
    ]
    for cp in loads:
        cp.start()
    loads[0].wait()
    loads[1].wait()
    G[z, c, x] = jnp.concatenate([tokv[...].astype(F32), grdv[...].astype(F32)], axis=0).astype(BF16)
    pl.semaphore_wait(barrier, len(peers))

    def block(dz, b):
        return G.at[zi(dz), c, xi(-b)]

    def along_z(way, hop, b):
        ref = block(-way * (hop - 1), b)
        i = 0 if way > 0 else 1
        send(ref, ref, z_s.at[i, hop - 1, b], z_r.at[i, hop - 1, b], dev(dz=way))

    def from_z(way, hop, b):
        i = 0 if way > 0 else 1
        arrived(block(-way * hop, b), z_s.at[i, hop - 1, b], z_r.at[i, hop - 1, b])

    def to_core(dz):
        ref = G.at[zi(dz), c]
        send(ref, ref, c_s.at[dz + 3], c_r.at[dz + 3], dev(dc=1))

    def from_core(dz):
        arrived(G.at[zi(dz), 1 - c], c_s.at[dz + 3], c_r.at[dz + 3])

    own = block(0, 0)
    along_z(1, 1, 0)
    along_z(-1, 1, 0)
    for b in (1, 3, 2):
        send(own, own, xs_s.at[b - 1], xs_r.at[b - 1], dev(dx=b))

    for i in range(3):
        loads[2 + i].wait()
        loads[5 + i].wait()
        keep = expand(mv[i], row * UNITS, y * FEATS)
        KEEP[i] = keep.astype(BF16)
        WE[i, :UNITS] = (wv[i].astype(F32) * keep).astype(BF16)
        WE[i, UNITS:] = jnp.zeros((PAD - UNITS, FEATS), BF16)

    for b in (1, 3, 2):
        arrived(block(0, b), xs_s.at[b - 1], xs_r.at[b - 1])
        along_z(1, 1, b)
        along_z(-1, 1, b)
    to_core(0)

    def goes(way, hop, b):
        return hop <= 3 or (hop == 4 and (b < 2) == (way > 0))

    def ring(hop):
        for b in (0, 1, 3, 2):
            for way in (-1, 1):
                if goes(way, hop, b):
                    from_z(way, hop, b)
                    if goes(way, hop + 1, b) and hop < 4:
                        along_z(way, hop + 1, b)
        if hop < 4:
            to_core(hop)
            to_core(-hop)
        else:
            to_core(4)

    def partial(g):
        toks, grds = [], []
        for d in GROUPS[g]:
            from_core(d)
            v = G[zi(d)].astype(F32)
            toks.append(v[:, :, :8].reshape(64, FEATS))
            grds.append(v[:, :, 8:].reshape(64, FEATS))
        t = jnp.concatenate(toks, axis=0).astype(BF16)
        r = jnp.concatenate(grds, axis=0).astype(BF16)
        TOKS[g * 128 : g * 128 + 128] = t
        GRDS[g * 128 : g * 128 + 128] = r
        nt = (((1,), (1,)), ((), ()))
        for i, v in enumerate((t, t, r)):
            P32[g, :, :, i * PAD : (i + 1) * PAD] = lax.dot_general(
                v, WE[i], nt, preferred_element_type=F32
            ).reshape(NY, 16, PAD)
        SP[g, 0] = P32[g, yi(1)].astype(BF16)
        SP[g, 1] = P32[g, yi(3)].astype(BF16)
        send(SP.at[g], RP.at[g], y1_s.at[g, 0], y1_r.at[g, 0], dev(dy=1))
        SM[g, 0] = P32[g, yi(-1)].astype(BF16)
        SM[g, 1] = P32[g, yi(-3)].astype(BF16)
        send(SM.at[g], RM.at[g], y1_s.at[g, 1], y1_r.at[g, 1], dev(dy=-1))
        S2[g] = P32[g, yi(4)].astype(BF16)
        send(S2.at[g], R2.at[g], y1_s.at[g, 2], y1_r.at[g, 2], dev(dy=2 if g % 2 == 0 else -2))

    def relay(g):
        arrived(RP.at[g], y1_s.at[g, 0], y1_r.at[g, 0])
        arrived(RM.at[g], y1_s.at[g, 1], y1_r.at[g, 1])
        arrived(R2.at[g], y1_s.at[g, 2], y1_r.at[g, 2])
        up = P32[g, yi(2)] + RP[g, 1].astype(F32)
        down = P32[g, yi(-2)] + RM[g, 1].astype(F32)
        far = R2[g].astype(F32)
        if g % 2 == 0:
            up = up + far
        else:
            down = down + far
        SB[g] = up.astype(BF16)
        send(SB.at[g], RB.at[g], y2_s.at[g, 0], y2_r.at[g, 0], dev(dy=2))
        SA[g] = down.astype(BF16)
        send(SA.at[g], RA.at[g], y2_s.at[g, 1], y2_r.at[g, 1], dev(dy=-2))

    def owned(g):
        arrived(RB.at[g], y2_s.at[g, 0], y2_r.at[g, 0])
        arrived(RA.at[g], y2_s.at[g, 1], y2_r.at[g, 1])
        total = (
            P32[g, y]
            + (RP[g, 0].astype(F32) + RM[g, 0].astype(F32))
            + (RB[g].astype(F32) + RA[g].astype(F32))
        )
        gate, upper, dhid = total[:, :PAD], total[:, PAD : 2 * PAD], total[:, 2 * PAD :]
        sig = jax.nn.sigmoid(gate)
        act = gate * sig
        hidden = act * upper
        dup = dhid * act
        dgate = dhid * upper * sig * (1.0 + gate * (1.0 - sig))
        D[g, y] = jnp.concatenate([hidden, dgate, dup], axis=1).astype(BF16)
        ref = D.at[g, y]
        for i, k in enumerate((2, -2, 1, -1)):
            send(ref, ref, d_s.at[g, i], d_r.at[g, i], dev(dy=k))

    def spread(g):
        low, high = D.at[g, yi(-2)], D.at[g, yi(2)]
        arrived(low, d_s.at[g, 0], d_r.at[g, 0])
        send(low, low, e_s.at[g, 0], e_r.at[g, 0], dev(dy=1))
        if g % 2 == 0:
            send(low, low, e_s.at[g, 2], e_r.at[g, 2], dev(dy=2))
        arrived(high, d_s.at[g, 1], d_r.at[g, 1])
        send(high, high, e_s.at[g, 1], e_r.at[g, 1], dev(dy=-1))
        if g % 2 == 1:
            send(high, high, e_s.at[g, 2], e_r.at[g, 2], dev(dy=-2))

    def back(g):
        arrived(D.at[g, yi(-1)], d_s.at[g, 2], d_r.at[g, 2])
        arrived(D.at[g, yi(1)], d_s.at[g, 3], d_r.at[g, 3])
        arrived(D.at[g, yi(-3)], e_s.at[g, 0], e_r.at[g, 0])
        arrived(D.at[g, yi(3)], e_s.at[g, 1], e_r.at[g, 1])
        arrived(D.at[g, yi(4)], e_s.at[g, 2], e_r.at[g, 2])
        pair = D[g].reshape(128, WIDE)
        total = jnp.dot(pair[:, PAD : 2 * PAD], WE[0], preferred_element_type=F32) + jnp.dot(
            pair[:, 2 * PAD :], WE[1], preferred_element_type=F32
        )
        total = total.reshape(2, 2, NX, 8, FEATS)
        for s in range(2):
            for k in range(2):
                GTS[g, k, s] = total[s, k]
        send(GTS.at[g, 1 - c], GR.at[g], g_s.at[g], g_r.at[g], dev(dc=1))

    def over_x(g):
        arrived(GR.at[g], g_s.at[g], g_r.at[g])

        def mine(k):
            return [GTS[g, c, s, xi(k)] + GR[g, s, xi(k)] for s in range(2)]

        for k in (2, 1, 3):
            XS[g, k - 1] = jnp.concatenate(mine(k), axis=0).astype(BF16)
            send(XS.at[g, k - 1], XR.at[g, k - 1], h_s.at[g, k - 1], h_r.at[g, k - 1], dev(dx=k))
        KX[g] = jnp.concatenate(mine(0), axis=0)

    def over_z(g):
        total = KX[g]
        for k in (1, 3, 2):
            arrived(XR.at[g, k - 1], h_s.at[g, k - 1], h_r.at[g, k - 1])
            total = total + XR[g, k - 1].astype(F32)
        for s, d in enumerate(GROUPS[g]):
            part = total[s * 8 : s * 8 + 8]
            if d == 0:
                ZO[...] = part
            else:
                i = d + 3
                ZS[i] = part
                send(ZS.at[i], ZR.at[i], k_s.at[i], k_r.at[i], dev(dz=d))

    def weights(i, out):
        other = (GRDS, TOKS, TOKS)[i]
        full = lax.dot_general(
            D[...].reshape(512, WIDE)[:, i * PAD : (i + 1) * PAD],
            other[...],
            (((0,), (0,)), ((), ())),
            preferred_element_type=F32,
        )
        out[...] = (full[:UNITS] * KEEP[(2, 0, 1)[i]].astype(F32)).astype(BF16)

    ring(1)
    partial(0)
    ring(2)
    partial(1)
    relay(0)
    ring(3)
    partial(2)
    relay(1)
    owned(0)
    ring(4)
    partial(3)
    relay(2)
    owned(1)
    spread(0)
    relay(3)
    owned(2)
    spread(1)
    back(0)
    owned(3)
    spread(2)
    back(1)
    over_x(0)
    spread(3)
    back(2)
    over_x(1)
    over_z(0)
    back(3)
    over_x(2)
    over_z(1)
    weights(0, o_d)
    over_x(3)
    over_z(2)
    weights(1, o_g)
    over_z(3)
    weights(2, o_u)
    total = ZO[...]
    for d in (1, -1, 2, -2, 3, -3, 4):
        arrived(ZR.at[d + 3], k_s.at[d + 3], k_r.at[d + 3])
        total = total + ZR[d + 3]
    o_t[...] = total.astype(BF16)
    for cp in sends:
        cp.wait_send()


def shards(tokens, out_grad, w_gate, w_up, w_down, mask_gate, mask_up, mask_down):
    vm = pltpu.VMEM
    dma = pltpu.SemaphoreType.DMA
    n = len(GROUPS)
    scratch = [
        vm((8, FEATS), BF16), vm((8, FEATS), BF16), vm((3, UNITS, FEATS), BF16),
        vm((3,) + mask_gate.shape, jnp.int32),
        vm((NZ, 2, NX, 16, FEATS), BF16), vm((3, PAD, FEATS), BF16), vm((3, UNITS, FEATS), BF16),
        vm((512, FEATS), BF16), vm((512, FEATS), BF16), vm((n, NY, 16, WIDE), F32),
        vm((n, 2, 16, WIDE), BF16), vm((n, 2, 16, WIDE), BF16), vm((n, 16, WIDE), BF16),
        vm((n, 2, 16, WIDE), BF16), vm((n, 2, 16, WIDE), BF16), vm((n, 16, WIDE), BF16),
        vm((n, 16, WIDE), BF16), vm((n, 16, WIDE), BF16), vm((n, 16, WIDE), BF16), vm((n, 16, WIDE), BF16),
        vm((n, NY, 16, WIDE), BF16),
        vm((n, 2, 2, NX, 8, FEATS), F32), vm((n, 2, NX, 8, FEATS), F32),
        vm((n, 3, 16, FEATS), BF16), vm((n, 3, 16, FEATS), BF16), vm((n, 16, FEATS), F32),
        vm((8, 8, FEATS), F32), vm((8, 8, FEATS), F32), vm((8, FEATS), F32),
        dma((8,)),
        dma((3,)), dma((3,)), dma((2, 4, 4)), dma((2, 4, 4)), dma((8,)), dma((8,)),
        dma((n, 3)), dma((n, 3)), dma((n, 2)), dma((n, 2)), dma((n, 4)), dma((n, 4)),
        dma((n, 3)), dma((n, 3)), dma((n,)), dma((n,)), dma((n, 3)), dma((n, 3)), dma((8,)), dma((8,)),
    ]
    outs = [jax.ShapeDtypeStruct(tokens.shape, BF16)] + [
        jax.ShapeDtypeStruct(w_gate.shape, BF16) for _ in range(3)
    ]
    return pl.pallas_call(
        kernel,
        out_shape=outs,
        in_specs=[pl.BlockSpec(memory_space=pl.ANY)] * 8,
        out_specs=[pl.BlockSpec(memory_space=pltpu.VMEM)] * 4,
        scratch_shapes=scratch,
        compiler_params=pltpu.CompilerParams(
            collective_id=0, has_side_effects=True, vmem_limit_bytes=40 * 1024 * 1024
        ),
        name="ffn_backward",
    )(tokens, out_grad, w_gate, w_up, w_down, mask_gate, mask_up, mask_down)


def solution(mesh):
    spec = P("row", "col")
    return jax.shard_map(
        shards,
        mesh=mesh,
        in_specs=(spec,) * 5 + (P(),) * 3,
        out_specs=(spec,) * 4,
        check_vma=False,
    )
```

time: 552 us -> 76.4 us (0.14)
  blocking collectives: 268 us -> 0 us
  waiting for transfers between devices: 243 us -> 0 us
  Pallas kernels: 0 us -> 66 us
  matrix products: 16.6 us -> 0 us
  between operations: 14.5 us -> 0.68 us
    unnamed x1 -> x0, blocking collectives: 268 us -> none
    all_gather x2 -> x0, waiting for transfers between devices: 167 us -> none  [the longest x1 86.3 us: shards(): lax.all_gather(out_grad, 'row', axis=0, tiled=True)]
    psum x1 -> x0, waiting for transfers between devices: 74.4 us -> none  [shards(): summed, dsummed = lax.psum((partial_value, dpartial), 'col')]
    pallas_call x0 -> x1, Pallas kernels: none -> 66 us  [shards(): pl.pallas_call(kernel, out_shape=outs, in_specs=[pl.BlockSpec(memory_spac...]
    dot_general x8 -> x0, matrix products: 16.6 us -> none  [the longest x3 4.7 us: expand(): return jnp.dot(inner, right.T)]
    unnamed x11 -> x21, local copies, waits for them, and re-layouts: 1.92 us -> 8.29 us
  transfers between devices with their start and end apart: 3 -> 0, of which waited for: 3 -> 0; matrix products, arithmetic and copies ran while one was open for 2% -> 0% of each run, Pallas kernels for 0% -> 0%
where the time goes in v1:
time: 76.4 us; the launch traced here: 74.9 us
  Pallas kernels  66 us (86%)
  local copies, waits for them, and re-layouts  8.29 us (11%)
    pallas_call x1, Pallas kernels, shards(): pl.pallas_call(kernel, out_shape=outs, in_specs=[pl.BlockSpec(memory_spac...  66 us
    unnamed x21, local copies, waits for them, and re-layouts  8.29 us

profile of v1, /device:TPU:1, one launch (start us, length us, event | category | flops | bytes accessed | tf_op | source)
XLA Modules:
  0.0 74.9 jit_solution(6464729441963337961)
XLA Ops:
  0.6 0.0 copy-start.5
  0.6 0.8 %copy.12.mg = s32[112,64]{1,0:T(8,128)S(1)} copy(s32[112,64]{0,1:T(8,128)} %param.13) | data formatting | bytes 57344 | tf_op args[5]
  1.5 0.0 copy-done.5
  1.5 0.0 copy-start.6
  1.5 0.1 copy.13.mu
  1.6 0.7 copy-done.6
  2.3 0.0 copy-start.3
  2.3 0.0 copy-start.4
  2.3 0.1 copy.14.md
  2.4 0.6 copy-done.3
  3.0 0.0 copy-done.4
  3.0 0.0 copy-start
  3.0 1.0 %copy-done = bf16[224,1024]{1,0:T(8,128)(2,1)S(1)} copy-done((bf16[224,1024]{1,0:T(8,128)(2,1)S(1)}, bf16[224,1024]{1,0:T(8,128)(2,1)}, u32[]{:S(2)}) %copy-start) | copy-done | bytes 458776
  4.0 0.0 copy-start.1
  4.0 1.0 %copy-done.1 = bf16[224,1024]{1,0:T(8,128)(2,1)S(1)} copy-done((bf16[224,1024]{1,0:T(8,128)(2,1)S(1)}, bf16[224,1024]{1,0:T(8,128)(2,1)}, u32[]{:S(2)}) %copy-start.1) | copy-done | bytes 458776
  5.0 0.0 copy-start.2
  5.0 1.0 %copy-done.2 = bf16[224,1024]{1,0:T(8,128)(2,1)S(1)} copy-done((bf16[224,1024]{1,0:T(8,128)(2,1)S(1)}, bf16[224,1024]{1,0:T(8,128)(2,1)}, u32[]{:S(2)}) %copy-start.2) | copy-done | bytes 458776
  6.1 66.0 %ffn_backward.1 = (bf16[8,1024]{1,0:T(8,128)(2,1)S(1)}, bf16[224,1024]{1,0:T(8,128)(2,1)S(1)}, bf16[224,1024]{1,0:T(8,128)(2,1)S(1)}, bf16[224,1024]{1,0:T(8,128)(2,1)S(1)}) custom-call(bf16[8,1024]{1,0:T(8,128)(2,1)S(1)} %copy-done.3, bf16[8,1024]{1,0:T(8,128)(2,1)S(1)} %copy-done.4, bf16[224,1024]{1,0:T(8,128)(2,1)S(1)} %copy-done, ...), custom_call_target="tpu_custom_call" | custom-call | tf_op jit(solution)/shard_map/ffn_backward/pallas_call | solution.py:336
  72.0 0.6 copy.19
  72.6 0.8 %copy.20 = bf16[224,1024]{1,0:T(8,128)(2,1)} copy(bf16[224,1024]{1,0:T(8,128)(2,1)S(1)} %get-tuple-element.9) | data formatting | bytes 917504
  73.4 0.8 %copy.21 = bf16[224,1024]{1,0:T(8,128)(2,1)} copy(bf16[224,1024]{1,0:T(8,128)(2,1)S(1)} %get-tuple-element.10) | data formatting | bytes 917504
  74.2 0.8 %copy.22 = bf16[224,1024]{1,0:T(8,128)(2,1)} copy(bf16[224,1024]{1,0:T(8,128)(2,1)S(1)} %get-tuple-element.11) | data formatting | bytes 917504
Async XLA Ops:
  0.6 0.9 %copy-start.5 = (s32[112,64]{0,1:T(8,128)S(1)}, s32[112,64]{0,1:T(8,128)}, u32[]{:S(2)}) copy-start(s32[112,64]{0,1:T(8,128)} %param.14) | copy-start | bytes 86020
  1.5 0.8 %copy-start.6 = (s32[112,64]{0,1:T(8,128)S(1)}, s32[112,64]{0,1:T(8,128)}, u32[]{:S(2)}) copy-start(s32[112,64]{0,1:T(8,128)} %param.15) | copy-start | bytes 86020
  2.3 0.7 copy-start.3
  2.3 0.7 copy-start.4
  3.0 1.0 %copy-start = (bf16[224,1024]{1,0:T(8,128)(2,1)S(1)}, bf16[224,1024]{1,0:T(8,128)(2,1)}, u32[]{:S(2)}) copy-start(bf16[224,1024]{1,0:T(8,128)(2,1)} %wg.1) | copy-start | bytes 1376260
  4.0 1.0 %copy-start.1 = (bf16[224,1024]{1,0:T(8,128)(2,1)S(1)}, bf16[224,1024]{1,0:T(8,128)(2,1)}, u32[]{:S(2)}) copy-start(bf16[224,1024]{1,0:T(8,128)(2,1)} %wu.1) | copy-start | bytes 1376260
  5.0 1.0 %copy-start.2 = (bf16[224,1024]{1,0:T(8,128)(2,1)S(1)}, bf16[224,1024]{1,0:T(8,128)(2,1)}, u32[]{:S(2)}) copy-start(bf16[224,1024]{1,0:T(8,128)(2,1)} %wd.1) | copy-start | bytes 1376260

commit v2 on v0

v2 whole, which is shorter than its diff:
```python
import jax
import jax.numpy as jnp
from jax import lax
from jax.experimental import pallas as pl
from jax.experimental.pallas import tpu as pltpu
from jax.sharding import PartitionSpec as P

NZ, NX, NY = 8, 4, 8
UNITS, FEATS, PAD = 224, 1024, 256
WIDE = 3 * PAD
TOKENS = 512
GROUPS = ((0,), (4,), (3,), (-3,), (2,), (-2,), (1,), (-1,))
N, S = len(GROUPS), len(GROUPS[0])
SLABS = tuple(o for g in GROUPS for o in g)
RO = 8 * S
F32, BF16 = jnp.float32, jnp.bfloat16
NN = (((1,), (0,)), ((), ()))
NT = (((1,), (1,)), ((), ()))
TN = (((0,), (0,)), ((), ()))


ORDER = (
    (2, 0), (2, 1), (2, 2), (1, 0), (0, 4), (3, 0), (0, 3), (0, -3), (0, 2), (0, -2),
    (0, 1), (0, -1), (1, 4), (4, 0), (3, 1), (1, 3), (1, -3), (5, 0), (3, 2), (1, 2),
    (3, 3), (4, 1), (1, -2), (3, 4), (6, 0), (1, 1), (4, 2), (3, 5), (4, 3), (1, -1),
    (3, 6), (5, 1), (4, 4), (3, 7), (7, 0), (5, 2), (4, 5), (5, 3), (8, 0), (4, 6),
    (6, 1), (5, 4), (4, 7), (6, 2), (9, 0), (5, 5), (6, 3), (5, 6), (7, 1), (6, 4),
    (5, 7), (7, 2), (8, 1), (6, 5), (7, 3), (6, 6), (8, 2), (7, 4), (6, 7), (8, 3),
    (10, 0), (9, 1), (7, 5), (8, 4), (7, 6), (9, 2), (8, 5), (9, 3), (7, 7), (8, 6),
    (12, 0), (9, 4), (8, 7), (11, 0), (9, 5), (9, 6), (9, 7), (13, 0),
)


def dot(a, b, dims):
    return lax.dot_general(a, b, dims, preferred_element_type=F32)


def expand(mask, row_start, col_start):
    wide, blocks = mask.shape
    unit = (row_start + lax.broadcasted_iota(jnp.int32, (UNITS, blocks), 0)) >> 7
    left = (unit == lax.broadcasted_iota(jnp.int32, (UNITS, blocks), 1)).astype(F32).astype(BF16)
    feat = (col_start + lax.broadcasted_iota(jnp.int32, (wide, FEATS), 1)) >> 7
    right = (feat == lax.broadcasted_iota(jnp.int32, (wide, FEATS), 0)).astype(F32).astype(BF16)
    inner = dot(left, mask.astype(F32).astype(BF16), NT)
    return dot(inner.astype(BF16), right, NN)


def kernel(
    tok, grd, wg, wu, wd, mg, mu, md,
    o_t, o_g, o_u, o_d,
    tokv, grdv, wv, mv, G, WE, WT, KEEP, TOKS, GRDS, P32,
    S1, R1, S3, R3, DG, DC, HID, GTS, GR, XS, XR, KX, ZS, ZR, ZO,
    lsem, out_sem, x_r, z_r, c_r, y1_r, y2_r, d_r, e_r, g_r, h_r, k_r, n_r,
):
    row, y = lax.axis_index("row"), lax.axis_index("col")
    c = lax.rem(row, 2)
    x = lax.rem(row // 2, NX)
    z = row // (2 * NX)

    def zi(d):
        return lax.rem(z + (d + NZ), NZ)

    def xi(d):
        return lax.rem(x + (d + NX), NX)

    def yi(d):
        return lax.rem(y + (d + NY), NY)

    def dev(dz=0, dx=0, dc=0, dy=0):
        return ((zi(dz) * NX + xi(dx)) * 2 + lax.rem(c + dc, 2), yi(dy))

    x_s, z_s, c_s, y1_s, y2_s, d_s, g_s, h_s, k_s, n_s = (out_sem.at[i] for i in range(10))

    def copy(src, dst, ssem, rsem, where):
        return pltpu.make_async_remote_copy(
            src, dst, ssem, rsem, device_id=where, device_id_type=pl.DeviceIdType.MESH
        )

    def send(src, dst, ssem, rsem, where):
        copy(src, dst, ssem, rsem, where).start()

    def arrived(ref, rsem):
        copy(ref, ref, out_sem.at[0], rsem, dev(dc=1)).wait_recv()

    def left(ref, ssem):
        copy(ref, ref, ssem, k_r.at[0], dev(dc=1)).wait_send()

    peers = (
        [dev(dc=1)]
        + [dev(dx=k) for k in (1, 2, 3)]
        + [dev(dz=k) for k in range(1, 8)]
        + [dev(dy=k) for k in range(1, 8)]
    )
    barrier = pltpu.get_barrier_semaphore()
    for p in peers:
        pl.semaphore_signal(barrier, inc=1, device_id=p, device_id_type=pl.DeviceIdType.MESH)
    loads = [
        pltpu.make_async_copy(s, d, lsem.at[i])
        for i, (s, d) in enumerate(
            (
                (tok, tokv), (grd, grdv),
                (mg, mv.at[0]), (mu, mv.at[1]), (md, mv.at[2]),
                (wg, wv.at[0]), (wu, wv.at[1]), (wd, wv.at[2]),
            )
        )
    ]
    for cp in loads:
        cp.start()
    loads[0].wait()
    loads[1].wait()
    G[z, c, x] = jnp.concatenate([tokv[...].astype(F32), grdv[...].astype(F32)], axis=0).astype(BF16)
    pl.semaphore_wait(barrier, len(peers))

    def over(o):
        ref = G.at[zi(o), c, x]
        for k in (1, 3, 2):
            send(ref, ref, x_s, x_r.at[o + 3], dev(dx=k))

    def fwd(o):
        i = (-o if o < 4 else 4) + 3
        arrived(G.at[zi(o), c, x], z_r.at[i])
        over(o)

    def slab(o):
        arrived(G.at[zi(o), c, 0:3], x_r.at[o + 3])
        ref = G.at[zi(o), c]
        send(ref, ref, c_s, c_r.at[o + 3], dev(dc=1))

    own = G.at[z, c, x]
    over(0)
    for d in (4, -3, 3, -2, 2, -1, 1):
        send(own, own, z_s, z_r.at[d + 3], dev(dz=d))

    def prep(i):
        loads[2 + i].wait()
        loads[5 + i].wait()
        keep = expand(mv[i], row * UNITS, y * FEATS)
        KEEP[i] = keep.astype(BF16)
        eff = jnp.concatenate(
            [(wv[i].astype(F32) * keep).astype(BF16), jnp.zeros((PAD - UNITS, FEATS), BF16)], axis=0
        )
        WE[i * PAD : (i + 1) * PAD] = eff
        WT[:, i * PAD : (i + 1) * PAD] = eff.T

    def partial(g):
        toks, grds = [], []
        for o in GROUPS[g]:
            arrived(G.at[zi(o), 1 - c], c_r.at[o + 3])
            v = G[zi(o)].astype(F32)
            toks.append(v[:, :, :8].reshape(64, FEATS))
            grds.append(v[:, :, 8:].reshape(64, FEATS))
        t = jnp.concatenate(toks, axis=0).astype(BF16)
        r = jnp.concatenate(grds, axis=0).astype(BF16)
        at = slice(g * 64 * S, (g + 1) * 64 * S)
        TOKS[at] = t
        GRDS[at] = r
        P32[g, :, :, : 2 * PAD] = dot(t, WT[:, : 2 * PAD], NN).reshape(NY, RO, 2 * PAD)
        P32[g, :, :, 2 * PAD :] = dot(r, WT[:, 2 * PAD :], NN).reshape(NY, RO, PAD)
        for i, k in enumerate((1, 3, -1, -3, 4)):
            S1[g, i] = P32[g, yi(k)].astype(BF16)
        send(S1.at[g, 0:2], R1.at[g, 0:2], y1_s, y1_r.at[g], dev(dy=1))
        send(S1.at[g, 2:4], R1.at[g, 2:4], y1_s, y1_r.at[g], dev(dy=-1))
        send(S1.at[g, 4], R1.at[g, 4], y1_s, y1_r.at[g], dev(dy=2 if g % 2 == 0 else -2))

    def relay(g):
        arrived(R1.at[g], y1_r.at[g])
        up = P32[g, yi(2)] + R1[g, 1].astype(F32)
        down = P32[g, yi(-2)] + R1[g, 3].astype(F32)
        far = R1[g, 4].astype(F32)
        if g % 2 == 0:
            up = up + far
        else:
            down = down + far
        S3[g, 0] = up.astype(BF16)
        send(S3.at[g, 0], R3.at[g, 0], y2_s, y2_r.at[g], dev(dy=2))
        S3[g, 1] = down.astype(BF16)
        send(S3.at[g, 1], R3.at[g, 1], y2_s, y2_r.at[g], dev(dy=-2))

    def owned(g):
        arrived(R3.at[g], y2_r.at[g])
        total = (
            P32[g, y]
            + (R1[g, 0].astype(F32) + R1[g, 2].astype(F32))
            + (R3[g, 0].astype(F32) + R3[g, 1].astype(F32))
        )
        gate, upper, dhid = total[:, :PAD], total[:, PAD : 2 * PAD], total[:, 2 * PAD :]
        sig = jax.nn.sigmoid(gate)
        act = gate * sig
        dgate = dhid * upper * sig * (1.0 + gate * (1.0 - sig))
        DG[g, y] = jnp.concatenate([dgate, dhid * act], axis=1).astype(BF16)
        ref = DG.at[g, y]
        send(ref, ref, d_s, d_r.at[g, 0], dev(dy=2))
        send(ref, ref, d_s, d_r.at[g, 1], dev(dy=-2))
        send(ref, ref, d_s, e_r.at[g], dev(dy=1))
        send(ref, ref, d_s, e_r.at[g], dev(dy=-1))
        HID[y, g] = (act * upper).astype(BF16)

    def hid(_):
        ref = HID.at[y]
        send(ref, ref, n_s, n_r.at[0], dev(dy=2))
        send(ref, ref, n_s, n_r.at[1], dev(dy=-2))
        send(ref, ref, n_s, n_r.at[2], dev(dy=1))
        send(ref, ref, n_s, n_r.at[2], dev(dy=-1))

    def hid_spread(_):
        low, high = HID.at[yi(-2)], HID.at[yi(2)]
        arrived(low, n_r.at[0])
        send(low, low, n_s, n_r.at[2], dev(dy=1))
        send(low, low, n_s, n_r.at[2], dev(dy=2))
        arrived(high, n_r.at[1])
        send(high, high, n_s, n_r.at[2], dev(dy=-1))

    def spread(g):
        low, high = DG.at[g, yi(-2)], DG.at[g, yi(2)]
        arrived(low, d_r.at[g, 0])
        send(low, low, d_s, e_r.at[g], dev(dy=1))
        if g % 2 == 0:
            send(low, low, d_s, e_r.at[g], dev(dy=2))
        arrived(high, d_r.at[g, 1])
        send(high, high, d_s, e_r.at[g], dev(dy=-1))
        if g % 2 == 1:
            send(high, high, d_s, e_r.at[g], dev(dy=-2))

    def back(g):
        arrived(DG.at[g, 0:5], e_r.at[g])
        pair = DG[g].astype(F32).reshape(64 * S, 2 * PAD).astype(BF16)
        DC[g * 64 * S : (g + 1) * 64 * S] = pair
        total = dot(pair, WE[: 2 * PAD], NN).reshape(S, 2, NX, 8, FEATS)
        for s in range(S):
            for k in range(2):
                GTS[g, k, s] = total[s, k]
        send(GTS.at[g, 1 - c], GR.at[g], g_s, g_r.at[g], dev(dc=1))

    def over_x(g):
        arrived(GR.at[g], g_r.at[g])

        def mine(k):
            return jnp.concatenate([GTS[g, c, s, xi(k)] + GR[g, s, xi(k)] for s in range(S)], axis=0)

        for k in (2, 1, 3):
            XS[g, k - 1] = mine(k).astype(BF16)
            send(XS.at[g, k - 1], XR.at[g, k - 1], h_s, h_r.at[g], dev(dx=k))
        KX[g] = mine(0)

    def over_z(g):
        arrived(XR.at[g], h_r.at[g])
        total = KX[g] + XR[g, 0].astype(F32) + XR[g, 1].astype(F32) + XR[g, 2].astype(F32)
        for s, d in enumerate(GROUPS[g]):
            part = total[s * 8 : s * 8 + 8]
            if d == 0:
                ZO[...] = part
            else:
                i = d + 3
                ZS[i] = part
                send(ZS.at[i], ZR.at[i], k_s, k_r.at[0], dev(dz=d))

    def weights(i, left, right, out):
        out[...] = (dot(left, right[...], TN)[:UNITS] * KEEP[i].astype(F32)).astype(BF16)

    def pair_weights(_):
        weights(0, DC[:, :PAD], TOKS, o_g)
        weights(1, DC[:, PAD:], TOKS, o_u)

    def down_weights(_):
        arrived(HID.at[0:5], n_r.at[2])
        hidden = jnp.concatenate(
            [HID[:, g].astype(F32).reshape(64 * S, PAD) for g in range(N)], axis=0
        ).astype(BF16)
        weights(2, hidden, GRDS, o_d)

    stages = (
        fwd, slab, prep, partial, relay, owned, spread, back, over_x, over_z,
        hid, hid_spread, pair_weights, down_weights,
    )
    for stage, at in ORDER:
        stages[stage](at)
    arrived(ZR.at[0:7], k_r.at[0])
    total = ZO[...]
    for d in (1, -1, 2, -2, 3, -3, 4):
        total = total + ZR[d + 3]
    o_t[...] = total.astype(BF16)
    for ref, ssem in (
        (G.at[0:3], x_s), (G.at[0:7, 0, 0], z_s), (G.at[:, 0], c_s), (S1, y1_s), (S3, y2_s),
        (DG.at[:, 0:7], d_s), (GTS.at[:, 0], g_s), (XS, h_s), (ZS.at[0:7], k_s), (HID.at[0:7], n_s),
    ):
        left(ref, ssem)


def store(a, b, c, d, oa, ob, oc, od, sem):
    copies = [
        pltpu.make_async_copy(s, t, sem.at[i])
        for i, (s, t) in enumerate(((a, oa), (b, ob), (c, oc), (d, od)))
    ]
    for cp in copies:
        cp.start()
    for cp in copies:
        cp.wait()


def shards(tokens, out_grad, w_gate, w_up, w_down, mask_gate, mask_up, mask_down):
    vm = pltpu.VMEM
    dma = pltpu.SemaphoreType.DMA
    scratch = [
        vm((8, FEATS), BF16), vm((8, FEATS), BF16), vm((3, UNITS, FEATS), BF16),
        vm((3,) + mask_gate.shape[::-1], jnp.int32),
        vm((NZ, 2, NX, 16, FEATS), BF16), vm((WIDE, FEATS), BF16), vm((FEATS, WIDE), BF16),
        vm((3, UNITS, FEATS), BF16),
        vm((TOKENS, FEATS), BF16), vm((TOKENS, FEATS), BF16), vm((N, NY, RO, WIDE), F32),
        vm((N, 5, RO, WIDE), BF16), vm((N, 5, RO, WIDE), BF16), vm((N, 2, RO, WIDE), BF16), vm((N, 2, RO, WIDE), BF16),
        vm((N, NY, RO, 2 * PAD), BF16), vm((TOKENS, 2 * PAD), BF16), vm((NY, N, RO, PAD), BF16),
        vm((N, 2, S, NX, 8, FEATS), F32), vm((N, S, NX, 8, FEATS), F32),
        vm((N, 3, RO, FEATS), BF16), vm((N, 3, RO, FEATS), BF16), vm((N, RO, FEATS), F32),
        vm((8, 8, FEATS), F32), vm((8, 8, FEATS), F32), vm((8, FEATS), F32),
        dma((8,)),
        dma((10,)), dma((8,)), dma((8,)), dma((8,)), dma((N,)), dma((N,)), dma((N, 2)), dma((N,)),
        dma((N,)), dma((N,)), dma((1,)), dma((3,)),
    ]
    outs = [jax.ShapeDtypeStruct(tokens.shape, BF16)] + [
        jax.ShapeDtypeStruct(w_gate.shape, BF16) for _ in range(3)
    ]
    operands = [
        pltpu.with_memory_space_constraint(a, pltpu.HBM)
        for a in (tokens, out_grad, w_gate, w_up, w_down, mask_gate.T, mask_up.T, mask_down.T)
    ]
    results = pl.pallas_call(
        kernel,
        out_shape=outs,
        in_specs=[pl.BlockSpec(memory_space=pltpu.HBM)] * 8,
        out_specs=[pl.BlockSpec(memory_space=pltpu.VMEM)] * 4,
        scratch_shapes=scratch,
        compiler_params=pltpu.CompilerParams(
            collective_id=0, has_side_effects=True, vmem_limit_bytes=40 * 1024 * 1024
        ),
        name="ffn_backward",
    )(*operands)
    return pl.pallas_call(
        store,
        out_shape=outs,
        in_specs=[pl.BlockSpec(memory_space=pltpu.VMEM)] * 4,
        out_specs=[pl.BlockSpec(memory_space=pltpu.HBM)] * 4,
        scratch_shapes=[dma((4,))],
        compiler_params=pltpu.CompilerParams(vmem_limit_bytes=8 * 1024 * 1024),
        name="store_results",
    )(*results)


def solution(mesh):
    spec = P("row", "col")
    return jax.shard_map(
        shards,
        mesh=mesh,
        in_specs=(spec,) * 5 + (P(),) * 3,
        out_specs=(spec,) * 4,
        check_vma=False,
    )
```

time: 552 us -> 64.4 us (0.12)
  blocking collectives: 268 us -> 0 us
  waiting for transfers between devices: 243 us -> 0 us
  Pallas kernels: 0 us -> 63.5 us
  matrix products: 16.6 us -> 0 us
  between operations: 14.5 us -> 0.64 us
    unnamed x1 -> x0, blocking collectives: 268 us -> none
    all_gather x2 -> x0, waiting for transfers between devices: 167 us -> none  [the longest x1 86.3 us: shards(): lax.all_gather(out_grad, 'row', axis=0, tiled=True)]
    psum x1 -> x0, waiting for transfers between devices: 74.4 us -> none  [shards(): summed, dsummed = lax.psum((partial_value, dpartial), 'col')]
    pallas_call x0 -> x2, Pallas kernels: none -> 63.5 us  [the longest x1 62.4 us: shards(): pl.pallas_call(kernel, out_shape=outs, in_specs=[pl.BlockSpec(memory_spac...]
    dot_general x8 -> x0, matrix products: 16.6 us -> none  [the longest x3 4.7 us: expand(): return jnp.dot(inner, right.T)]
  transfers between devices with their start and end apart: 3 -> 0, of which waited for: 3 -> 0; matrix products, arithmetic and copies ran while one was open for 2% -> 0% of each run, Pallas kernels for 0% -> 0%
where the time goes in v2:
time: 64.4 us; the launch traced here: 64.1 us
  Pallas kernels  63.5 us (99%)
    pallas_call x1, Pallas kernels, shards(): pl.pallas_call(kernel, out_shape=outs, in_specs=[pl.BlockSpec(memory_spac...  62.4 us

profile of v2, /device:TPU:1, one launch (start us, length us, event | category | flops | bytes accessed | tf_op | source)
XLA Modules:
  0.0 64.1 jit_solution(860501577042491128)
XLA Ops:
  0.6 62.4 %ffn_backward.1 = (bf16[8,1024]{1,0:T(8,128)(2,1)S(1)}, bf16[224,1024]{1,0:T(8,128)(2,1)S(1)}, bf16[224,1024]{1,0:T(8,128)(2,1)S(1)}, bf16[224,1024]{1,0:T(8,128)(2,1)S(1)}) custom-call(bf16[8,1024]{1,0:T(8,128)(2,1)} %tok.1, bf16[8,1024]{1,0:T(8,128)(2,1)} %grd.1, bf16[224,1024]{1,0:T(8,128)(2,1)} %wg.1, bf16[224,1024]{1,0:T(8,128)(2,1)} %wu.1, ...), custom_call_target="tpu_custom_call" | custom-call | tf_op jit(solution)/shard_map/ffn_backward/pallas_call | solution.py:325
  63.0 1.1 %store_results.1 = (bf16[8,1024]{1,0:T(8,128)(2,1)}, bf16[224,1024]{1,0:T(8,128)(2,1)}, bf16[224,1024]{1,0:T(8,128)(2,1)}, bf16[224,1024]{1,0:T(8,128)(2,1)}) custom-call(bf16[8,1024]{1,0:T(8,128)(2,1)S(1)} %get-tuple-element.8.a, bf16[224,1024]{1,0:T(8,128)(2,1)S(1)} %get-tuple-element.9.b, bf16[224,1024]{1,0:T(8,128)(2,1)S(1)} %get-tuple-element.10.c, ...), custom_call_target="tpu_custom_call" | custom-call | tf_op jit(solution)/shard_map/store_results/pallas_call | solution.py:336

commit v3 on v2

--- a/solution.py
+++ b/solution.py
@@ -9,7 +9,7 @@
 UNITS, FEATS, PAD = 224, 1024, 256
 WIDE = 3 * PAD
 TOKENS = 512
-GROUPS = ((0,), (4,), (3,), (-3,), (2,), (-2,), (1,), (-1,))
+GROUPS = ((0,), (4,), (1,), (-1,), (3,), (-3,), (2,), (-2,))
 N, S = len(GROUPS), len(GROUPS[0])
 SLABS = tuple(o for g in GROUPS for o in g)
 RO = 8 * S
@@ -21,13 +21,13 @@
 
 ORDER = (
     (2, 0), (2, 1), (2, 2), (1, 0), (0, 4), (3, 0), (0, 3), (0, -3), (0, 2), (0, -2),
-    (0, 1), (0, -1), (1, 4), (4, 0), (3, 1), (1, 3), (1, -3), (5, 0), (3, 2), (1, 2),
-    (3, 3), (4, 1), (1, -2), (3, 4), (6, 0), (1, 1), (4, 2), (3, 5), (4, 3), (1, -1),
-    (3, 6), (5, 1), (4, 4), (3, 7), (7, 0), (5, 2), (4, 5), (5, 3), (8, 0), (4, 6),
-    (6, 1), (5, 4), (4, 7), (6, 2), (9, 0), (5, 5), (6, 3), (5, 6), (7, 1), (6, 4),
-    (5, 7), (7, 2), (8, 1), (6, 5), (7, 3), (6, 6), (8, 2), (7, 4), (6, 7), (8, 3),
-    (10, 0), (9, 1), (7, 5), (8, 4), (7, 6), (9, 2), (8, 5), (9, 3), (7, 7), (8, 6),
-    (12, 0), (9, 4), (8, 7), (11, 0), (9, 5), (9, 6), (9, 7), (13, 0),
+    (1, 4), (4, 0), (1, 1), (1, -1), (3, 1), (1, 3), (3, 2), (3, 3), (1, -3), (3, 4),
+    (5, 0), (1, 2), (3, 5), (4, 1), (1, -2), (3, 6), (4, 2), (4, 3), (3, 7), (4, 4),
+    (6, 0), (4, 5), (5, 1), (4, 6), (5, 2), (5, 3), (4, 7), (5, 4), (7, 0), (5, 5),
+    (6, 1), (5, 6), (6, 2), (8, 0), (6, 3), (5, 7), (6, 4), (6, 5), (7, 1), (6, 6),
+    (9, 0), (7, 2), (7, 3), (6, 7), (8, 1), (7, 4), (8, 2), (7, 5), (8, 3), (7, 6),
+    (8, 4), (10, 0), (8, 5), (9, 1), (7, 7), (8, 6), (9, 2), (12, 0), (8, 7), (9, 3),
+    (9, 4), (9, 5), (11, 0), (9, 6), (9, 7), (13, 0),
 )
 
 
@@ -89,7 +89,7 @@
         [dev(dc=1)]
         + [dev(dx=k) for k in (1, 2, 3)]
         + [dev(dz=k) for k in range(1, 8)]
-        + [dev(dy=k) for k in range(1, 8)]
+        + [dev(dy=k) for k in (1, 2, -1, -2)]
     )
     barrier = pltpu.get_barrier_semaphore()
     for p in peers:
@@ -122,13 +122,19 @@
         over(o)
 
     def slab(o):
-        arrived(G.at[zi(o), c, 0:3], x_r.at[o + 3])
         ref = G.at[zi(o), c]
+        if abs(o) == 1:
+            arrived(ref, z_r.at[3 - o])
+        else:
+            arrived(G.at[zi(o), c, 0:3], x_r.at[o + 3])
         send(ref, ref, c_s, c_r.at[o + 3], dev(dc=1))
+        if o == 0:
+            for d in (1, -1):
+                send(ref, ref, c_s, z_r.at[d + 3], dev(dz=d))
 
     own = G.at[z, c, x]
     over(0)
-    for d in (4, -3, 3, -2, 2, -1, 1):
+    for d in (4, -3, 3, -2, 2):
         send(own, own, z_s, z_r.at[d + 3], dev(dz=d))
 
     def prep(i):
@@ -280,7 +286,7 @@
         total = total + ZR[d + 3]
     o_t[...] = total.astype(BF16)
     for ref, ssem in (
-        (G.at[0:3], x_s), (G.at[0:7, 0, 0], z_s), (G.at[:, 0], c_s), (S1, y1_s), (S3, y2_s),
+        (G.at[0:3, :, 0:3], x_s), (G.at[0:5, 0, 0], z_s), (G.at[0:5], c_s), (S1, y1_s), (S3, y2_s),
         (DG.at[:, 0:7], d_s), (GTS.at[:, 0], g_s), (XS, h_s), (ZS.at[0:7], k_s), (HID.at[0:7], n_s),
     ):
         left(ref, ssem)

time: 64.4 us -> 60.1 us (0.933)
  Pallas kernels: 63.5 us -> 59.3 us
    pallas_call x1, Pallas kernels: 62.4 us -> 58.2 us  [shards(): pl.pallas_call(kernel, out_shape=outs, in_specs=[pl.BlockSpec(memory_spac...]
where the time goes in v3:
time: 60.1 us; the launch traced here: 60 us
  Pallas kernels  59.3 us (99%)
  between operations  0.64 us (1%)
    pallas_call x1, Pallas kernels, shards(): pl.pallas_call(kernel, out_shape=outs, in_specs=[pl.BlockSpec(memory_spac...  58.2 us

profile of v3, /device:TPU:1, one launch (start us, length us, event | category | flops | bytes accessed | tf_op | source)
XLA Modules:
  0.0 60.0 jit_solution(4782198036522714211)
XLA Ops:
  0.6 58.2 %ffn_backward.1 = (bf16[8,1024]{1,0:T(8,128)(2,1)S(1)}, bf16[224,1024]{1,0:T(8,128)(2,1)S(1)}, bf16[224,1024]{1,0:T(8,128)(2,1)S(1)}, bf16[224,1024]{1,0:T(8,128)(2,1)S(1)}) custom-call(bf16[8,1024]{1,0:T(8,128)(2,1)} %tok.1, bf16[8,1024]{1,0:T(8,128)(2,1)} %grd.1, bf16[224,1024]{1,0:T(8,128)(2,1)} %wg.1, bf16[224,1024]{1,0:T(8,128)(2,1)} %wu.1, ...), custom_call_target="tpu_custom_call" | custom-call | tf_op jit(solution)/shard_map/ffn_backward/pallas_call | solution.py:331
  58.8 1.1 %store_results.1 = (bf16[8,1024]{1,0:T(8,128)(2,1)}, bf16[224,1024]{1,0:T(8,128)(2,1)}, bf16[224,1024]{1,0:T(8,128)(2,1)}, bf16[224,1024]{1,0:T(8,128)(2,1)}) custom-call(bf16[8,1024]{1,0:T(8,128)(2,1)S(1)} %get-tuple-element.8.a, bf16[224,1024]{1,0:T(8,128)(2,1)S(1)} %get-tuple-element.9.b, bf16[224,1024]{1,0:T(8,128)(2,1)S(1)} %get-tuple-element.10.c, ...), custom_call_target="tpu_custom_call" | custom-call | tf_op jit(solution)/shard_map/store_results/pallas_call | solution.py:342

commit v4 on v3

--- a/solution.py
+++ b/solution.py
@@ -85,15 +85,6 @@
     def left(ref, ssem):
         copy(ref, ref, ssem, k_r.at[0], dev(dc=1)).wait_send()
 
-    peers = (
-        [dev(dc=1)]
-        + [dev(dx=k) for k in (1, 2, 3)]
-        + [dev(dz=k) for k in range(1, 8)]
-        + [dev(dy=k) for k in (1, 2, -1, -2)]
-    )
-    barrier = pltpu.get_barrier_semaphore()
-    for p in peers:
-        pl.semaphore_signal(barrier, inc=1, device_id=p, device_id_type=pl.DeviceIdType.MESH)
     loads = [
         pltpu.make_async_copy(s, d, lsem.at[i])
         for i, (s, d) in enumerate(
@@ -104,7 +95,18 @@
             )
         )
     ]
-    for cp in loads:
+    loads[0].start()
+    loads[1].start()
+    peers = (
+        [dev(dz=k) for k in (4, 3, -3, 2, -2, 1, -1)]
+        + [dev(dx=k) for k in (2, 1, 3)]
+        + [dev(dy=k) for k in (2, -2, 1, -1)]
+        + [dev(dc=1)]
+    )
+    barrier = pltpu.get_barrier_semaphore()
+    for p in peers:
+        pl.semaphore_signal(barrier, inc=1, device_id=p, device_id_type=pl.DeviceIdType.MESH)
+    for cp in loads[2:]:
         cp.start()
     loads[0].wait()
     loads[1].wait()

time: 60.1 us -> 59.9 us (level)
  no operation moved by 1% of the time
where the time goes in v4:
time: 59.9 us; the launch traced here: 59.7 us
  Pallas kernels  59 us (98%)
  between operations  0.64 us (1%)
    pallas_call x1, Pallas kernels, shards(): pl.pallas_call(kernel, out_shape=outs, in_specs=[pl.BlockSpec(memory_spac...  57.9 us

profile of v4, /device:TPU:1, one launch (start us, length us, event | category | flops | bytes accessed | tf_op | source)
XLA Modules:
  0.0 59.7 jit_solution(15814967940929737988)
XLA Ops:
  0.6 57.9 %ffn_backward.1 = (bf16[8,1024]{1,0:T(8,128)(2,1)S(1)}, bf16[224,1024]{1,0:T(8,128)(2,1)S(1)}, bf16[224,1024]{1,0:T(8,128)(2,1)S(1)}, bf16[224,1024]{1,0:T(8,128)(2,1)S(1)}) custom-call(bf16[8,1024]{1,0:T(8,128)(2,1)} %tok.1, bf16[8,1024]{1,0:T(8,128)(2,1)} %grd.1, bf16[224,1024]{1,0:T(8,128)(2,1)} %wg.1, bf16[224,1024]{1,0:T(8,128)(2,1)} %wu.1, ...), custom_call_target="tpu_custom_call" | custom-call | tf_op jit(solution)/shard_map/ffn_backward/pallas_call | solution.py:333
  58.6 1.1 %store_results.1 = (bf16[8,1024]{1,0:T(8,128)(2,1)}, bf16[224,1024]{1,0:T(8,128)(2,1)}, bf16[224,1024]{1,0:T(8,128)(2,1)}, bf16[224,1024]{1,0:T(8,128)(2,1)}) custom-call(bf16[8,1024]{1,0:T(8,128)(2,1)S(1)} %get-tuple-element.8.a, bf16[224,1024]{1,0:T(8,128)(2,1)S(1)} %get-tuple-element.9.b, bf16[224,1024]{1,0:T(8,128)(2,1)S(1)} %get-tuple-element.10.c, ...), custom_call_target="tpu_custom_call" | custom-call | tf_op jit(solution)/shard_map/store_results/pallas_call | solution.py:344

commit v5 on v4

--- a/solution.py
+++ b/solution.py
@@ -26,8 +26,8 @@
     (6, 0), (4, 5), (5, 1), (4, 6), (5, 2), (5, 3), (4, 7), (5, 4), (7, 0), (5, 5),
     (6, 1), (5, 6), (6, 2), (8, 0), (6, 3), (5, 7), (6, 4), (6, 5), (7, 1), (6, 6),
     (9, 0), (7, 2), (7, 3), (6, 7), (8, 1), (7, 4), (8, 2), (7, 5), (8, 3), (7, 6),
-    (8, 4), (10, 0), (8, 5), (9, 1), (7, 7), (8, 6), (9, 2), (12, 0), (8, 7), (9, 3),
-    (9, 4), (9, 5), (11, 0), (9, 6), (9, 7), (13, 0),
+    (8, 4), (10, 0), (8, 5), (9, 1), (7, 7), (8, 6), (9, 2), (8, 7), (9, 3),
+    (9, 4), (9, 5), (11, 0), (9, 6), (9, 7), (12, 0), (13, 0),
 )
 
 

time: 59.9 us -> 60 us (level)
  no operation moved by 1% of the time
where the time goes in v5:
time: 60 us; the launch traced here: 59.8 us
  Pallas kernels  59.2 us (99%)
  between operations  0.64 us (1%)
    pallas_call x1, Pallas kernels, shards(): pl.pallas_call(kernel, out_shape=outs, in_specs=[pl.BlockSpec(memory_spac...  58.1 us

profile of v5, /device:TPU:1, one launch (start us, length us, event | category | flops | bytes accessed | tf_op | source)
XLA Modules:
  0.0 59.8 jit_solution(9337937392930740914)
XLA Ops:
  0.6 58.1 %ffn_backward.1 = (bf16[8,1024]{1,0:T(8,128)(2,1)S(1)}, bf16[224,1024]{1,0:T(8,128)(2,1)S(1)}, bf16[224,1024]{1,0:T(8,128)(2,1)S(1)}, bf16[224,1024]{1,0:T(8,128)(2,1)S(1)}) custom-call(bf16[8,1024]{1,0:T(8,128)(2,1)} %tok.1, bf16[8,1024]{1,0:T(8,128)(2,1)} %grd.1, bf16[224,1024]{1,0:T(8,128)(2,1)} %wg.1, bf16[224,1024]{1,0:T(8,128)(2,1)} %wu.1, ...), custom_call_target="tpu_custom_call" | custom-call | tf_op jit(solution)/shard_map/ffn_backward/pallas_call | solution.py:333
  58.7 1.1 %store_results.1 = (bf16[8,1024]{1,0:T(8,128)(2,1)}, bf16[224,1024]{1,0:T(8,128)(2,1)}, bf16[224,1024]{1,0:T(8,128)(2,1)}, bf16[224,1024]{1,0:T(8,128)(2,1)}) custom-call(bf16[8,1024]{1,0:T(8,128)(2,1)S(1)} %get-tuple-element.8.a, bf16[224,1024]{1,0:T(8,128)(2,1)S(1)} %get-tuple-element.9.b, bf16[224,1024]{1,0:T(8,128)(2,1)S(1)} %get-tuple-element.10.c, ...), custom_call_target="tpu_custom_call" | custom-call | tf_op jit(solution)/shard_map/store_results/pallas_call | solution.py:344

commit v6 on v4

--- a/solution.py
+++ b/solution.py
@@ -164,11 +164,12 @@
         GRDS[at] = r
         P32[g, :, :, : 2 * PAD] = dot(t, WT[:, : 2 * PAD], NN).reshape(NY, RO, 2 * PAD)
         P32[g, :, :, 2 * PAD :] = dot(r, WT[:, 2 * PAD :], NN).reshape(NY, RO, PAD)
-        for i, k in enumerate((1, 3, -1, -3, 4)):
-            S1[g, i] = P32[g, yi(k)].astype(BF16)
-        send(S1.at[g, 0:2], R1.at[g, 0:2], y1_s, y1_r.at[g], dev(dy=1))
-        send(S1.at[g, 2:4], R1.at[g, 2:4], y1_s, y1_r.at[g], dev(dy=-1))
+        S1[g, 4] = P32[g, yi(4)].astype(BF16)
         send(S1.at[g, 4], R1.at[g, 4], y1_s, y1_r.at[g], dev(dy=2 if g % 2 == 0 else -2))
+        for i, way in ((0, 1), (2, -1)):
+            S1[g, i] = P32[g, yi(way)].astype(BF16)
+            S1[g, i + 1] = P32[g, yi(3 * way)].astype(BF16)
+            send(S1.at[g, i : i + 2], R1.at[g, i : i + 2], y1_s, y1_r.at[g], dev(dy=way))
 
     def relay(g):
         arrived(R1.at[g], y1_r.at[g])

time: 59.9 us -> 60.1 us (level)
  no operation moved by 1% of the time
where the time goes in v6:
time: 60.1 us; the launch traced here: 59.9 us
  Pallas kernels  59.2 us (99%)
  between operations  0.64 us (1%)
    pallas_call x1, Pallas kernels, shards(): pl.pallas_call(kernel, out_shape=outs, in_specs=[pl.BlockSpec(memory_spac...  58.1 us

profile of v6, /device:TPU:1, one launch (start us, length us, event | category | flops | bytes accessed | tf_op | source)
XLA Modules:
  0.0 59.9 jit_solution(4857658948982157061)
XLA Ops:
  0.6 58.1 %ffn_backward.1 = (bf16[8,1024]{1,0:T(8,128)(2,1)S(1)}, bf16[224,1024]{1,0:T(8,128)(2,1)S(1)}, bf16[224,1024]{1,0:T(8,128)(2,1)S(1)}, bf16[224,1024]{1,0:T(8,128)(2,1)S(1)}) custom-call(bf16[8,1024]{1,0:T(8,128)(2,1)} %tok.1, bf16[8,1024]{1,0:T(8,128)(2,1)} %grd.1, bf16[224,1024]{1,0:T(8,128)(2,1)} %wg.1, bf16[224,1024]{1,0:T(8,128)(2,1)} %wu.1, ...), custom_call_target="tpu_custom_call" | custom-call | tf_op jit(solution)/shard_map/ffn_backward/pallas_call | solution.py:334
  58.8 1.1 %store_results.1 = (bf16[8,1024]{1,0:T(8,128)(2,1)}, bf16[224,1024]{1,0:T(8,128)(2,1)}, bf16[224,1024]{1,0:T(8,128)(2,1)}, bf16[224,1024]{1,0:T(8,128)(2,1)}) custom-call(bf16[8,1024]{1,0:T(8,128)(2,1)S(1)} %get-tuple-element.8.a, bf16[224,1024]{1,0:T(8,128)(2,1)S(1)} %get-tuple-element.9.b, bf16[224,1024]{1,0:T(8,128)(2,1)S(1)} %get-tuple-element.10.c, ...), custom_call_target="tpu_custom_call" | custom-call | tf_op jit(solution)/shard_map/store_results/pallas_call | solution.py:345
